TPU v7x, 32 devices: a whole 2x2x4 slice. The times are simulated.
32 devices in a mesh: groups: 2 (over x), box: 16 (over z, y, core).
Axes of the slice: x: 2, y: 2, z: 4, core: 2. Of those that a mesh axis runs over, the one named last changes fastest.
Arguments:
- currents: bfloat16 [2048, 2, 128], P(('groups', 'box')), parts along dimension 0, may hold values from -6 to 6
- near_blocks: bfloat16 [1024, 4, 2, 128, 128], P('box'), may hold values from -0.1875 to 0.1875
- near_off: int32 [1024, 4], P('box'), may hold values from -32 to 32, as said below
- radiation: bfloat16 [1024, 2, 128, 128], P('box'), may hold values from -0.375 to 0.375
- interp: bfloat16 [512, 128], replicated, may hold values from -0.5 to 0.5
- translators: float32 [316, 2, 512], replicated, may hold values from -0.3125 to 0.3125
- send_list: int32 [16, 16, 16], P('box'), may hold values from 0 to 63
- inter_slot: int32 [1024, 189], P('box'), may hold values from 0 to 255, as said below
- trans_id: int32 [1024, 189], P('box'), may hold values from 0 to 315
Outputs:
- product: bfloat16 [2048, 2, 128], P(('groups', 'box')), parts along dimension 0
There are 2 independent parts, one for each index of `groups`. A program takes and returns all parts, laid end to end along the dimension named above; an argument that names none is the same for every part. Nothing has to cross between parts.
Inputs may be any that keep to these rules, and one draw needn't show every extreme that they name: `near_off`: entry 0 of every box is 0 (its own block); offsets reach -32 and 32 on every device. `inter_slot`: each entry's sender lies within 3 device indices of the box's own device; slots from one such sender to one receiver are used up to a count of 1 to 16, slots from farther devices never; all 16 from a device to itself, and entry 0 of each box is a slot of its own device.
All inputs are finite; a program needn't handle non-finite values.
Results may differ from a plain program's by a relative error of at most 0.007.
Values may be sent and summed in bfloat16 or wider, within the bound.
A program may use at most 128 MiB of HBM per device.

v0:
```python
import jax
import jax.numpy as jnp
from jax import lax
from jax.sharding import PartitionSpec as P

block_entries = 27
reach_devices = 3


def extended(array, sides, width):
    for axis, dim in sides:
        size, length = (lax.axis_size(axis), array.shape[dim])
        up = [(i, (i + 1) % size) for i in range(size - 1)]
        down = [(j, i) for i, j in up]
        last = lax.slice_in_dim(array, length - width, length, axis=dim)
        leading = lax.slice_in_dim(array, 0, width, axis=dim)
        before = lax.ppermute(last, axis, up)
        after = lax.ppermute(leading, axis, down)
        array = jnp.concatenate([before, array, after], axis=dim)
    return array


def shifted(value, axis, steps):
    count = lax.axis_size(axis)
    leading, last = (max(0, -steps), min(count, count - steps))
    return lax.ppermute(value, axis, [(source, source + steps) for source in range(leading, last)])


def on_device(
    currents, near_blocks, near_off, radiation, interp, translators, send_list, inter_slot, trans_id
):
    box_count = currents.shape[0]
    rim_width = box_count // 2
    peer_count = lax.axis_size("box")
    samples = interp.shape[0]
    padded = extended(currents, (("box", 0),), rim_width)
    local_index = jnp.arange(box_count, dtype=jnp.int32)
    sources = padded[local_index[:, None] + rim_width + near_off]
    parts = jnp.einsum("bncij,bnej->bcei", near_blocks, sources, preferred_element_type=jnp.float32)
    near_field = jnp.stack(
        [parts[:, 0, 0] - parts[:, 1, 1], parts[:, 0, 1] + parts[:, 1, 0]], axis=1
    )
    parts = jnp.einsum("bcqm,bem->bceq", radiation, currents, preferred_element_type=jnp.float32)
    coarse = jnp.stack(
        [parts[:, 0, 0] - parts[:, 1, 1], parts[:, 0, 1] + parts[:, 1, 0]], axis=1
    ).astype(jnp.bfloat16)
    pattern = jnp.einsum("pq,bcq->bcp", interp, coarse, preferred_element_type=jnp.float32).astype(
        jnp.bfloat16
    )
    pattern_pieces = []
    list_pieces = []
    for offset in range(2 * reach_devices + 1):
        distance = reach_devices - offset
        if distance == 0:
            pattern_pieces.append(pattern)
            list_pieces.append(send_list)
        else:
            pattern_pieces.append(shifted(pattern, "box", distance))
            list_pieces.append(shifted(send_list, "box", distance))
    beside_all = jnp.concatenate(pattern_pieces, axis=0)
    lists = jnp.concatenate(list_pieces, axis=0)
    own = lax.axis_index("box")
    mine = lax.dynamic_index_in_dim(lists, own, 1, keepdims=False)
    peers = jnp.arange(peer_count, dtype=jnp.int32)
    offsets = jnp.clip(peers - own + reach_devices, 0, 2 * reach_devices)
    rows_wanted = (offsets[:, None] * box_count + mine[offsets]).reshape(-1)
    received = beside_all[rows_wanted]

    def translate(step, total):
        first_entry = step * block_entries
        slots = lax.dynamic_slice_in_dim(inter_slot, first_entry, block_entries, 1)
        kinds = lax.dynamic_slice_in_dim(trans_id, first_entry, block_entries, 1)
        pats = received[slots].astype(jnp.float32)
        shifts = translators[kinds]
        real_part = jnp.sum(
            shifts[:, :, 0] * pats[:, :, 0] - shifts[:, :, 1] * pats[:, :, 1], axis=1
        )
        imag_part = jnp.sum(
            shifts[:, :, 0] * pats[:, :, 1] + shifts[:, :, 1] * pats[:, :, 0], axis=1
        )
        return total + jnp.stack([real_part, imag_part], axis=1)

    start_total = jnp.zeros((box_count, 2, samples), jnp.float32)
    incoming = lax.fori_loop(
        0, inter_slot.shape[1] // block_entries, translate, start_total
    ).astype(jnp.bfloat16)
    coarse_in = jnp.einsum(
        "pq,bcp->bcq", interp, incoming, preferred_element_type=jnp.float32
    ).astype(jnp.bfloat16)
    parts = jnp.einsum("bcqm,beq->bcem", radiation, coarse_in, preferred_element_type=jnp.float32)
    far_field = jnp.stack(
        [parts[:, 0, 0] + parts[:, 1, 1], parts[:, 0, 1] - parts[:, 1, 0]], axis=1
    )
    return (near_field + far_field).astype(jnp.bfloat16)


def solution(mesh):
    return jax.shard_map(
        on_device,
        mesh=mesh,
        in_specs=(
            P(("groups", "box"), None, None),
            P("box", None, None, None, None),
            P("box", None),
            P("box", None, None, None),
            P(),
            P(),
            P("box", None, None),
            P("box", None),
            P("box", None),
        ),
        out_specs=P(("groups", "box"), None, None),
        check_vma=False,
    )
```

profile of v0, /device:TPU:0, one launch (start us, length us, event | category | flops | bytes accessed | tf_op | source)
XLA Modules:
  0.0 437.2 jit_solution(9000170440606752416)
XLA Ops:
  0.0 2.5 collective-permute-start.10
  2.5 1.3 collective-permute-start.11
  3.8 1.3 collective-permute-start.12
  5.1 1.3 collective-permute-start.13
  6.4 7.8 %collective-permute-start.8 = (s32[1,16,16]{2,0,1:T(1,128)}, s32[1,16,16]{2,0,1:T(1,128)S(1)}, u32[]{:S(2)}, u32[]{:S(2)}) collective-permute-start(s32[1,16,16]{2,0,1:T(1,128)} %bitcast.78), channel_id=1, source_target_pairs={{0,3},{1,4},{2,5},{3,6},{4,7},{5,8},{6,9},{7,10},{8,11},{9,12},{10... | collective-permute-start | bytes 3080 | tf_op jit(solution)/shard_map/ppermute | solution.py:26
  15.0 3.4 convolution_bitcast_fusion.1
  19.0 4.8 %collective-permute-start.9 = (s32[1,16,16]{2,0,1:T(1,128)S(1)}, s32[1,16,16]{2,0,1:T(1,128)S(1)}, u32[]{:S(2)}, u32[]{:S(2)}) collective-permute-start(s32[1,16,16]{2,0,1:T(1,128)S(1)} %bitcast.79), channel_id=1, source_target_pairs={{0,2},{1,3},{2,4},{3,5},{4,6},{5,7},{6,8},{7,9},{8,10},{9,11},{10,... | collective-permute-start | bytes 3080 | tf_op jit(solution)/shard_map/ppermute | solution.py:26
  23.8 3.2 collective-permute-start.2
  27.1 3.4 collective-permute-start.3
  30.5 2.5 collective-permute-start.4
  33.0 3.0 collective-permute-start
  36.1 1.3 collective-permute-start.1
  38.3 1.3 collective-permute-start.5
  40.1 1.3 collective-permute-start.6
  42.4 8.1 %convolution_bitcast_fusion = f32[64,2,2,128]{3,2,1,0:T(2,128)S(1)} fusion(bf16[64,4,2,128,1]{3,2,4,1,0:T(2,128)(2,1)S(1)} %bitcast.69, bf16[64,4,2,128,128]{4,3,2,1,0:T(8,128)(2,1)} %param.12), kind=kOutput, calls=%fused_computation.13 | convolution fusion | flops 33554432 | bytes 17039360 | tf_op jit(solution)/shard_map/bncij,bnej->bcei/dot_general | solution.py:39
  51.3 1.3 collective-permute-start.7
  52.7 7.6 %collective-permute-done.7 = bf16[64,2,512]{2,0,1:T(8,128)(2,1)S(1)} collective-permute-done((bf16[64,2,512]{2,0,1:T(8,128)(2,1)S(1)}, bf16[64,2,512]{2,0,1:T(8,128)(2,1)S(1)}, u32[]{:S(2)}, u32[]{:S(2)}) %collective-permute-start.7) | collective-permute-done | bytes 131104 | tf_op jit(solution)/shard_map/ppermute | solution.py:26
  61.3 1.7 gather_fusion.4
  63.1 370.3 %while.14 = (s32[]{:T(128)}, f32[64,2,512]{2,1,0:T(2,128)S(1)}, s32[64,189]{1,0:T(8,128)S(1)}, f32[316,2,512]{2,1,0:T(2,128)S(1)}, s32[64,189]{1,0:T(8,128)S(1)}...) while((s32[]{:T(128)}, f32[64,2,512]{2,1,0:T(2,128)S(1)}, ...), condition=%wide.region_3.4_spmd.clone, body=%wide.region_0.3_spmd.clone.sunk | while | flops 8992903 | bytes 47678624 | solution.py:84
  63.5 11.0 %gather_fusion = bf16[1728,2,512]{2,1,0:T(2,128)(2,1)} fusion(bf16[256,2,512]{2,1,0:T(2,128)(2,1)S(1)} %get-tuple-element.239, s32[2048]{0:T(1024)S(1)} %pad_clamp_fusion.7), kind=kCustom, calls=%fused_computation.1.clone.clone.1 | custom fusion | bytes 7084800 | tf_op jit(solution)/shard_map/while/body/eval_jaxpr/gather | solution.py:73
  74.5 7.3 %convert.25 = f32[64,27,2,512]{3,2,1,0:T(2,128)} convert(bf16[64,27,2,512]{3,2,1,0:T(2,128)(2,1)} %bitcast.68) | non-fusion elementwise | flops 1769472 | bytes 10616832 | tf_op jit(solution)/shard_map/while/body/eval_jaxpr/convert_element_type | solution.py:73
  81.9 11.2 %gather_fusion.1 = f32[1728,2,512]{2,1,0:T(2,128)} fusion(f32[316,2,512]{2,1,0:T(2,128)S(1)} %get-tuple-element.237, s32[2048]{0:T(1024)S(1)} %pad_clamp_fusion.8), kind=kCustom, calls=%fused_computation.clone.clone.1 | custom fusion | bytes 14162688 | tf_op jit(solution)/shard_map/while/body/eval_jaxpr/gather | solution.py:74
  93.1 22.2 %subtract_reduce_fusion.2 = (f32[64,512]{1,0:T(8,128)S(1)}, f32[64,512]{1,0:T(8,128)S(1)}) fusion(f32[64,27,2,512]{3,2,1,0:T(2,128)} %convert.25, f32[64,27,2,512]{3,2,1,0:T(2,128)} %bitcast.67), kind=kLoop, calls=%fused_computation.6.clone.1 | loop fusion | flops 7012352 | bytes 14417920 | tf_op jit(solution)/shard_map/while/body/eval_jaxpr/reduce_sum | solution.py:75
  116.4 11.0 %gather_fusion = bf16[1728,2,512]{2,1,0:T(2,128)(2,1)} fusion(bf16[256,2,512]{2,1,0:T(2,128)(2,1)S(1)} %get-tuple-element.239, s32[2048]{0:T(1024)S(1)} %pad_clamp_fusion.7), kind=kCustom, calls=%fused_computation.1.clone.clone.1 | custom fusion | bytes 7084800 | tf_op jit(solution)/shard_map/while/body/eval_jaxpr/gather | solution.py:73
  127.4 7.3 %convert.25 = f32[64,27,2,512]{3,2,1,0:T(2,128)} convert(bf16[64,27,2,512]{3,2,1,0:T(2,128)(2,1)} %bitcast.68) | non-fusion elementwise | flops 1769472 | bytes 10616832 | tf_op jit(solution)/shard_map/while/body/eval_jaxpr/convert_element_type | solution.py:73
  134.8 11.2 %gather_fusion.1 = f32[1728,2,512]{2,1,0:T(2,128)} fusion(f32[316,2,512]{2,1,0:T(2,128)S(1)} %get-tuple-element.237, s32[2048]{0:T(1024)S(1)} %pad_clamp_fusion.8), kind=kCustom, calls=%fused_computation.clone.clone.1 | custom fusion | bytes 14162688 | tf_op jit(solution)/shard_map/while/body/eval_jaxpr/gather | solution.py:74
  146.0 22.2 %subtract_reduce_fusion.2 = (f32[64,512]{1,0:T(8,128)S(1)}, f32[64,512]{1,0:T(8,128)S(1)}) fusion(f32[64,27,2,512]{3,2,1,0:T(2,128)} %convert.25, f32[64,27,2,512]{3,2,1,0:T(2,128)} %bitcast.67), kind=kLoop, calls=%fused_computation.6.clone.1 | loop fusion | flops 7012352 | bytes 14417920 | tf_op jit(solution)/shard_map/while/body/eval_jaxpr/reduce_sum | solution.py:75
  169.2 11.0 %gather_fusion = bf16[1728,2,512]{2,1,0:T(2,128)(2,1)} fusion(bf16[256,2,512]{2,1,0:T(2,128)(2,1)S(1)} %get-tuple-element.239, s32[2048]{0:T(1024)S(1)} %pad_clamp_fusion.7), kind=kCustom, calls=%fused_computation.1.clone.clone.1 | custom fusion | bytes 7084800 | tf_op jit(solution)/shard_map/while/body/eval_jaxpr/gather | solution.py:73
  180.2 7.3 %convert.25 = f32[64,27,2,512]{3,2,1,0:T(2,128)} convert(bf16[64,27,2,512]{3,2,1,0:T(2,128)(2,1)} %bitcast.68) | non-fusion elementwise | flops 1769472 | bytes 10616832 | tf_op jit(solution)/shard_map/while/body/eval_jaxpr/convert_element_type | solution.py:73
  187.7 11.2 %gather_fusion.1 = f32[1728,2,512]{2,1,0:T(2,128)} fusion(f32[316,2,512]{2,1,0:T(2,128)S(1)} %get-tuple-element.237, s32[2048]{0:T(1024)S(1)} %pad_clamp_fusion.8), kind=kCustom, calls=%fused_computation.clone.clone.1 | custom fusion | bytes 14162688 | tf_op jit(solution)/shard_map/while/body/eval_jaxpr/gather | solution.py:74
  198.8 22.2 %subtract_reduce_fusion.2 = (f32[64,512]{1,0:T(8,128)S(1)}, f32[64,512]{1,0:T(8,128)S(1)}) fusion(f32[64,27,2,512]{3,2,1,0:T(2,128)} %convert.25, f32[64,27,2,512]{3,2,1,0:T(2,128)} %bitcast.67), kind=kLoop, calls=%fused_computation.6.clone.1 | loop fusion | flops 7012352 | bytes 14417920 | tf_op jit(solution)/shard_map/while/body/eval_jaxpr/reduce_sum | solution.py:75
  222.1 11.0 %gather_fusion = bf16[1728,2,512]{2,1,0:T(2,128)(2,1)} fusion(bf16[256,2,512]{2,1,0:T(2,128)(2,1)S(1)} %get-tuple-element.239, s32[2048]{0:T(1024)S(1)} %pad_clamp_fusion.7), kind=kCustom, calls=%fused_computation.1.clone.clone.1 | custom fusion | bytes 7084800 | tf_op jit(solution)/shard_map/while/body/eval_jaxpr/gather | solution.py:73
  233.1 7.3 %convert.25 = f32[64,27,2,512]{3,2,1,0:T(2,128)} convert(bf16[64,27,2,512]{3,2,1,0:T(2,128)(2,1)} %bitcast.68) | non-fusion elementwise | flops 1769472 | bytes 10616832 | tf_op jit(solution)/shard_map/while/body/eval_jaxpr/convert_element_type | solution.py:73
  240.6 11.2 %gather_fusion.1 = f32[1728,2,512]{2,1,0:T(2,128)} fusion(f32[316,2,512]{2,1,0:T(2,128)S(1)} %get-tuple-element.237, s32[2048]{0:T(1024)S(1)} %pad_clamp_fusion.8), kind=kCustom, calls=%fused_computation.clone.clone.1 | custom fusion | bytes 14162688 | tf_op jit(solution)/shard_map/while/body/eval_jaxpr/gather | solution.py:74
  251.7 22.2 %subtract_reduce_fusion.2 = (f32[64,512]{1,0:T(8,128)S(1)}, f32[64,512]{1,0:T(8,128)S(1)}) fusion(f32[64,27,2,512]{3,2,1,0:T(2,128)} %convert.25, f32[64,27,2,512]{3,2,1,0:T(2,128)} %bitcast.67), kind=kLoop, calls=%fused_computation.6.clone.1 | loop fusion | flops 7012352 | bytes 14417920 | tf_op jit(solution)/shard_map/while/body/eval_jaxpr/reduce_sum | solution.py:75
  275.0 11.0 %gather_fusion = bf16[1728,2,512]{2,1,0:T(2,128)(2,1)} fusion(bf16[256,2,512]{2,1,0:T(2,128)(2,1)S(1)} %get-tuple-element.239, s32[2048]{0:T(1024)S(1)} %pad_clamp_fusion.7), kind=kCustom, calls=%fused_computation.1.clone.clone.1 | custom fusion | bytes 7084800 | tf_op jit(solution)/shard_map/while/body/eval_jaxpr/gather | solution.py:73
  286.0 7.3 %convert.25 = f32[64,27,2,512]{3,2,1,0:T(2,128)} convert(bf16[64,27,2,512]{3,2,1,0:T(2,128)(2,1)} %bitcast.68) | non-fusion elementwise | flops 1769472 | bytes 10616832 | tf_op jit(solution)/shard_map/while/body/eval_jaxpr/convert_element_type | solution.py:73
  293.4 11.2 %gather_fusion.1 = f32[1728,2,512]{2,1,0:T(2,128)} fusion(f32[316,2,512]{2,1,0:T(2,128)S(1)} %get-tuple-element.237, s32[2048]{0:T(1024)S(1)} %pad_clamp_fusion.8), kind=kCustom, calls=%fused_computation.clone.clone.1 | custom fusion | bytes 14162688 | tf_op jit(solution)/shard_map/while/body/eval_jaxpr/gather | solution.py:74
  304.6 22.2 %subtract_reduce_fusion.2 = (f32[64,512]{1,0:T(8,128)S(1)}, f32[64,512]{1,0:T(8,128)S(1)}) fusion(f32[64,27,2,512]{3,2,1,0:T(2,128)} %convert.25, f32[64,27,2,512]{3,2,1,0:T(2,128)} %bitcast.67), kind=kLoop, calls=%fused_computation.6.clone.1 | loop fusion | flops 7012352 | bytes 14417920 | tf_op jit(solution)/shard_map/while/body/eval_jaxpr/reduce_sum | solution.py:75
  327.8 11.0 %gather_fusion = bf16[1728,2,512]{2,1,0:T(2,128)(2,1)} fusion(bf16[256,2,512]{2,1,0:T(2,128)(2,1)S(1)} %get-tuple-element.239, s32[2048]{0:T(1024)S(1)} %pad_clamp_fusion.7), kind=kCustom, calls=%fused_computation.1.clone.clone.1 | custom fusion | bytes 7084800 | tf_op jit(solution)/shard_map/while/body/eval_jaxpr/gather | solution.py:73
  338.8 7.3 %convert.25 = f32[64,27,2,512]{3,2,1,0:T(2,128)} convert(bf16[64,27,2,512]{3,2,1,0:T(2,128)(2,1)} %bitcast.68) | non-fusion elementwise | flops 1769472 | bytes 10616832 | tf_op jit(solution)/shard_map/while/body/eval_jaxpr/convert_element_type | solution.py:73
  346.3 11.2 %gather_fusion.1 = f32[1728,2,512]{2,1,0:T(2,128)} fusion(f32[316,2,512]{2,1,0:T(2,128)S(1)} %get-tuple-element.237, s32[2048]{0:T(1024)S(1)} %pad_clamp_fusion.8), kind=kCustom, calls=%fused_computation.clone.clone.1 | custom fusion | bytes 14162688 | tf_op jit(solution)/shard_map/while/body/eval_jaxpr/gather | solution.py:74
  357.4 22.2 %subtract_reduce_fusion.2 = (f32[64,512]{1,0:T(8,128)S(1)}, f32[64,512]{1,0:T(8,128)S(1)}) fusion(f32[64,27,2,512]{3,2,1,0:T(2,128)} %convert.25, f32[64,27,2,512]{3,2,1,0:T(2,128)} %bitcast.67), kind=kLoop, calls=%fused_computation.6.clone.1 | loop fusion | flops 7012352 | bytes 14417920 | tf_op jit(solution)/shard_map/while/body/eval_jaxpr/reduce_sum | solution.py:75
  380.7 11.0 %gather_fusion = bf16[1728,2,512]{2,1,0:T(2,128)(2,1)} fusion(bf16[256,2,512]{2,1,0:T(2,128)(2,1)S(1)} %get-tuple-element.239, s32[2048]{0:T(1024)S(1)} %pad_clamp_fusion.7), kind=kCustom, calls=%fused_computation.1.clone.clone.1 | custom fusion | bytes 7084800 | tf_op jit(solution)/shard_map/while/body/eval_jaxpr/gather | solution.py:73
  391.7 7.3 %convert.25 = f32[64,27,2,512]{3,2,1,0:T(2,128)} convert(bf16[64,27,2,512]{3,2,1,0:T(2,128)(2,1)} %bitcast.68) | non-fusion elementwise | flops 1769472 | bytes 10616832 | tf_op jit(solution)/shard_map/while/body/eval_jaxpr/convert_element_type | solution.py:73
  399.2 11.2 %gather_fusion.1 = f32[1728,2,512]{2,1,0:T(2,128)} fusion(f32[316,2,512]{2,1,0:T(2,128)S(1)} %get-tuple-element.237, s32[2048]{0:T(1024)S(1)} %pad_clamp_fusion.8), kind=kCustom, calls=%fused_computation.clone.clone.1 | custom fusion | bytes 14162688 | tf_op jit(solution)/shard_map/while/body/eval_jaxpr/gather | solution.py:74
  410.3 22.2 %subtract_reduce_fusion.2 = (f32[64,512]{1,0:T(8,128)S(1)}, f32[64,512]{1,0:T(8,128)S(1)}) fusion(f32[64,27,2,512]{3,2,1,0:T(2,128)} %convert.25, f32[64,27,2,512]{3,2,1,0:T(2,128)} %bitcast.67), kind=kLoop, calls=%fused_computation.6.clone.1 | loop fusion | flops 7012352 | bytes 14417920 | tf_op jit(solution)/shard_map/while/body/eval_jaxpr/reduce_sum | solution.py:75
  433.6 2.8 fusion.13
  (123 shorter events, 14.2 us)
Async XLA Ops:
  0.0 18.7 %copy-start = (bf16[512,128]{1,0:T(8,128)(2,1)S(1)}, bf16[512,128]{1,0:T(8,128)(2,1)}, u32[]{:S(2)}) copy-start(bf16[512,128]{1,0:T(8,128)(2,1)} %param.15) | copy-start | bytes 393220
  0.0 19.0 %copy-start.6 = (s32[1,16,16]{2,1,0:T(8,128)S(1)}, s32[1,16,16]{2,1,0:T(8,128)}, u32[]{:S(2)}) copy-start(s32[1,16,16]{2,1,0:T(8,128)} %param.17) | copy-start | bytes 3076
  0.0 41.4 %copy-start.4 = (bf16[64,2,128]{2,1,0:T(2,128)(2,1)S(1)}, bf16[64,2,128]{2,1,0:T(2,128)(2,1)}, u32[]{:S(2)}) copy-start(bf16[64,2,128]{2,1,0:T(2,128)(2,1)} %param.11) | copy-start | bytes 98308
  0.0 18.5 %copy-start.7 = (s32[64,4]{0,1:T(4,128)S(1)}, s32[64,4]{0,1:T(4,128)}, u32[]{:S(2)}) copy-start(s32[64,4]{0,1:T(4,128)} %param.13) | copy-start | bytes 3076
  0.0 18.9 %collective-permute-start.10 = (s32[1,16,16]{2,0,1:T(1,128)}, s32[1,16,16]{2,0,1:T(1,128)S(1)}, u32[]{:S(2)}, u32[]{:S(2)}) collective-permute-start(s32[1,16,16]{2,0,1:T(1,128)} %bitcast.74), channel_id=1, source_target_pairs={{0,1},{1,2},{2,3},{3,4},{4,5},{5,6},{6,7},{7,8},{8,9},{9,10},{10,1... | collective-permute-start | bytes 3080 | tf_op jit(solution)/shard_map/ppermute | solution.py:26
  2.5 21.3 %collective-permute-start.11 = (s32[1,16,16]{2,0,1:T(1,128)}, s32[1,16,16]{2,0,1:T(1,128)S(1)}, u32[]{:S(2)}, u32[]{:S(2)}) collective-permute-start(s32[1,16,16]{2,0,1:T(1,128)} %bitcast.75), channel_id=1, source_target_pairs={{1,0},{2,1},{3,2},{4,3},{5,4},{6,5},{7,6},{8,7},{9,8},{10,9},{11,1... | collective-permute-start | bytes 3080 | tf_op jit(solution)/shard_map/ppermute | solution.py:26
  3.8 23.2 %collective-permute-start.12 = (s32[1,16,16]{2,0,1:T(1,128)}, s32[1,16,16]{2,0,1:T(1,128)S(1)}, u32[]{:S(2)}, u32[]{:S(2)}) collective-permute-start(s32[1,16,16]{2,0,1:T(1,128)} %bitcast.76), channel_id=1, source_target_pairs={{2,0},{3,1},{4,2},{5,3},{6,4},{7,5},{8,6},{9,7},{10,8},{11,9},{12,... | collective-permute-start | bytes 3080 | tf_op jit(solution)/shard_map/ppermute | solution.py:26
  5.1 25.4 %collective-permute-start.13 = (s32[1,16,16]{2,0,1:T(1,128)}, s32[1,16,16]{2,0,1:T(1,128)S(1)}, u32[]{:S(2)}, u32[]{:S(2)}) collective-permute-start(s32[1,16,16]{2,0,1:T(1,128)} %bitcast.77), channel_id=1, source_target_pairs={{3,0},{4,1},{5,2},{6,3},{7,4},{8,5},{9,6},{10,7},{11,8},{12,9},{13... | collective-permute-start | bytes 3080 | tf_op jit(solution)/shard_map/ppermute | solution.py:26
  6.4 26.6 %collective-permute-start.8 = (s32[1,16,16]{2,0,1:T(1,128)}, s32[1,16,16]{2,0,1:T(1,128)S(1)}, u32[]{:S(2)}, u32[]{:S(2)}) collective-permute-start(s32[1,16,16]{2,0,1:T(1,128)} %bitcast.78), channel_id=1, source_target_pairs={{0,3},{1,4},{2,5},{3,6},{4,7},{5,8},{6,9},{7,10},{8,11},{9,12},{10... | collective-permute-start | bytes 3080 | tf_op jit(solution)/shard_map/ppermute | solution.py:26
  19.0 17.1 %collective-permute-start.9 = (s32[1,16,16]{2,0,1:T(1,128)S(1)}, s32[1,16,16]{2,0,1:T(1,128)S(1)}, u32[]{:S(2)}, u32[]{:S(2)}) collective-permute-start(s32[1,16,16]{2,0,1:T(1,128)S(1)} %bitcast.79), channel_id=1, source_target_pairs={{0,2},{1,3},{2,4},{3,5},{4,6},{5,7},{6,8},{7,9},{8,10},{9,11},{10,... | collective-permute-start | bytes 3080 | tf_op jit(solution)/shard_map/ppermute | solution.py:26
  23.8 27.4 %collective-permute-start.2 = (bf16[64,2,512]{2,0,1:T(8,128)(2,1)S(1)}, bf16[64,2,512]{2,0,1:T(8,128)(2,1)S(1)}, u32[]{:S(2)}, u32[]{:S(2)}) collective-permute-start(bf16[64,2,512]{2,0,1:T(8,128)(2,1)S(1)} %convolution_convert_fusion), channel_id=1, source_target_pairs={{0,3},{1,4},{2,5},{3,6},{4,7},{5,8},{6,9},{7,10},{8,11},{9,12},{10... | collective-permute-start | bytes 393224 | tf_op jit(solution)/shard_map/ppermute | solution.py:26
  27.1 25.5 %collective-permute-start.3 = (bf16[64,2,512]{2,0,1:T(8,128)(2,1)S(1)}, bf16[64,2,512]{2,0,1:T(8,128)(2,1)S(1)}, u32[]{:S(2)}, u32[]{:S(2)}) collective-permute-start(bf16[64,2,512]{2,0,1:T(8,128)(2,1)S(1)} %convolution_convert_fusion), channel_id=1, source_target_pairs={{0,2},{1,3},{2,4},{3,5},{4,6},{5,7},{6,8},{7,9},{8,10},{9,11},{10,... | collective-permute-start | bytes 393224 | tf_op jit(solution)/shard_map/ppermute | solution.py:26
  30.5 22.1 %collective-permute-start.4 = (bf16[64,2,512]{2,0,1:T(8,128)(2,1)S(1)}, bf16[64,2,512]{2,0,1:T(8,128)(2,1)S(1)}, u32[]{:S(2)}, u32[]{:S(2)}) collective-permute-start(bf16[64,2,512]{2,0,1:T(8,128)(2,1)S(1)} %convolution_convert_fusion), channel_id=1, source_target_pairs={{0,1},{1,2},{2,3},{3,4},{4,5},{5,6},{6,7},{7,8},{8,9},{9,10},{10,1... | collective-permute-start | bytes 393224 | tf_op jit(solution)/shard_map/ppermute | solution.py:26
  33.0 5.2 %collective-permute-start = (bf16[32,2,128]{2,1,0:T(2,128)(2,1)S(1)}, bf16[32,2,128]{2,1,0:T(2,128)(2,1)S(1)}, u32[]{:S(2)}, u32[]{:S(2)}) collective-permute-start(bf16[32,2,128]{2,1,0:T(2,128)(2,1)S(1)} %get-tuple-element.165), channel_id=1, source_target_pairs={{0,1},{1,2},{2,3},{3,4},{4,5},{5,6},{6,7},{7,8},{8,9},{9,10},{10,1... | collective-permute-start | bytes 49160 | tf_op jit(solution)/shard_map/ppermute | solution.py:17
  36.1 4.0 collective-permute-start.1
  38.3 14.4 %collective-permute-start.5 = (bf16[64,2,512]{2,0,1:T(8,128)(2,1)S(1)}, bf16[64,2,512]{2,0,1:T(8,128)(2,1)S(1)}, u32[]{:S(2)}, u32[]{:S(2)}) collective-permute-start(bf16[64,2,512]{2,0,1:T(8,128)(2,1)S(1)} %convolution_convert_fusion), channel_id=1, source_target_pairs={{1,0},{2,1},{3,2},{4,3},{5,4},{6,5},{7,6},{8,7},{9,8},{10,9},{11,1... | collective-permute-start | bytes 393224 | tf_op jit(solution)/shard_map/ppermute | solution.py:26
  40.1 12.6 %collective-permute-start.6 = (bf16[64,2,512]{2,0,1:T(8,128)(2,1)S(1)}, bf16[64,2,512]{2,0,1:T(8,128)(2,1)S(1)}, u32[]{:S(2)}, u32[]{:S(2)}) collective-permute-start(bf16[64,2,512]{2,0,1:T(8,128)(2,1)S(1)} %convolution_convert_fusion), channel_id=1, source_target_pairs={{2,0},{3,1},{4,2},{5,3},{6,4},{7,5},{8,6},{9,7},{10,8},{11,9},{12,... | collective-permute-start | bytes 393224 | tf_op jit(solution)/shard_map/ppermute | solution.py:26
  50.5 12.5 %copy-start.1 = (f32[316,2,512]{2,1,0:T(2,128)S(1)}, f32[316,2,512]{2,1,0:T(2,128)}, u32[]{:S(2)}) copy-start(f32[316,2,512]{2,1,0:T(2,128)} %param.16) | copy-start | bytes 3883012
  50.5 12.5 %copy-start.2 = (s32[64,189]{1,0:T(8,128)S(1)}, s32[64,189]{1,0:T(8,128)}, u32[]{:S(2)}) copy-start(s32[64,189]{1,0:T(8,128)} %param.19) | copy-start | bytes 145156
  50.5 12.5 %copy-start.3 = (s32[64,189]{1,0:T(8,128)S(1)}, s32[64,189]{1,0:T(8,128)}, u32[]{:S(2)}) copy-start(s32[64,189]{1,0:T(8,128)} %param.18) | copy-start | bytes 145156
  51.3 9.1 %collective-permute-start.7 = (bf16[64,2,512]{2,0,1:T(8,128)(2,1)S(1)}, bf16[64,2,512]{2,0,1:T(8,128)(2,1)S(1)}, u32[]{:S(2)}, u32[]{:S(2)}) collective-permute-start(bf16[64,2,512]{2,0,1:T(8,128)(2,1)S(1)} %convolution_convert_fusion), channel_id=1, source_target_pairs={{3,0},{4,1},{5,2},{6,3},{7,4},{8,5},{9,6},{10,7},{11,8},{12,9},{13... | collective-permute-start | bytes 393224 | tf_op jit(solution)/shard_map/ppermute | solution.py:26
  433.3 3.2 copy-start.5
where the time goes:
time: 440 us; the launch traced here: 437 us
  other arithmetic  212 us (48%)
  local copies, waits for them, and re-layouts  164 us (37%)
  starting transfers between devices  36.3 us (8%)
  matrix products  14.7 us (3%)
  waiting for transfers between devices  8.16 us (2%)
    reduce_sum x7, other arithmetic, translate(): jnp.sum(shifts[:, :, 0] * pats[:, :, 0] - shifts[:, :, 1] * pats[:, :, 1]...  156 us
    gather x7, local copies, waits for them, and re-layouts, translate(): shifts = translators[kinds]  78.1 us
    gather x7, local copies, waits for them, and re-layouts, translate(): pats = received[slots].astype(jnp.float32)  77 us
    convert_element_type x7, other arithmetic, translate(): pats = received[slots].astype(jnp.float32)  51 us
    ppermute x12, starting transfers between devices, shifted(): lax.ppermute(value, axis, [(source, source + steps) for source in range(l...  32 us
  transfers between devices with their start and end apart: 14, of which 2 were waited for; matrix products, arithmetic and copies ran while one was open for 4% of the time, Pallas kernels for 0%

commit v1 on v0

v1 whole, which is shorter than its diff:
```python
import functools

import jax
import jax.numpy as jnp
from jax import lax
from jax.experimental import pallas as pl
from jax.experimental.pallas import tpu as pltpu
from jax.sharding import PartitionSpec as P

reach = 3
span = 2 * reach + 1
rows_box = 8
lane = 128
half, full = jnp.bfloat16, jnp.float32


def dot(a, b):
    return lax.dot_general(a, b, (((1,), (0,)), ((), ())), preferred_element_type=full)


def dot_t(a, b):
    return lax.dot_general(a, b, (((1,), (1,)), ((), ())), preferred_element_type=full)


def iota(shape, dim):
    return lax.broadcasted_iota(jnp.int32, shape, dim)


def one_hot(condition):
    return jnp.where(condition, 1.0, 0.0).astype(half)


def turned(value):
    count = value.shape[0]
    even = (iota(value.shape, 0) & 1) == 0
    return jnp.where(even, -pltpu.roll(value, count - 1, 0), pltpu.roll(value, 1, 0))


def kernel(
    groups, peers, near_chunks, rad_chunks, batch,
    cur_ref, near_hbm, off_ref, rad_hbm, interp_ref, trans_hbm, list_ref, slot_ref, kind_ref,
    out_ref,
    near, rad, trans, table, src, near_sum, far_sum, spread, coarse_sum, outgoing, arrived,
    counts, pats, slots, kinds, inc, back, stage, result,
    near_sem, rad_sem, trans_sem, cur_send, cur_recv, pat_send, pat_recv, res_send, res_recv,
):
    group, place = lax.axis_index("groups"), lax.axis_index("box")
    boxes = rad.shape[0]
    mine = near.shape[0]
    rim = boxes // 2
    cap = outgoing.shape[2]
    first = group * mine
    samples = interp_ref.shape[0]
    blocks = samples // lane
    entries = slot_ref.shape[1]
    table_rows = table.shape[1]

    def device(shift, turn):
        return (lax.rem(group + turn, groups), lax.rem(place + shift + peers, peers))

    others = [
        (shift, turn)
        for turn in range(groups)
        for shift in range(-reach, reach + 1)
        if (shift, turn) != (0, 0)
    ]
    barrier = pltpu.get_barrier_semaphore()
    for shift, turn in others:
        pl.semaphore_signal(
            barrier, inc=1, device_id=device(shift, turn), device_id_type=pl.DeviceIdType.MESH
        )

    rad_step, near_step = boxes // rad_chunks, mine // near_chunks
    rad_copies = [
        pltpu.make_async_copy(
            rad_hbm.at[pl.ds(q * rad_step, rad_step)],
            rad.at[pl.ds(q * rad_step, rad_step)],
            rad_sem.at[q],
        )
        for q in range(rad_chunks)
    ]
    near_copies = [
        pltpu.make_async_copy(
            near_hbm.at[pl.ds(first + q * near_step, near_step)],
            near.at[pl.ds(q * near_step, near_step)],
            near_sem.at[q],
        )
        for q in range(near_chunks)
    ]
    trans_copy = pltpu.make_async_copy(trans_hbm, trans, trans_sem)
    for copy in rad_copies + [trans_copy] + near_copies:
        copy.start()

    pl.semaphore_wait(barrier, len(others))

    inner = 2 * boxes
    edge = 2 * rim
    parts = {
        1: (pl.ds(inner - edge, edge), pl.ds(0, edge)),
        0: (pl.ds(0, inner), pl.ds(edge, inner)),
        -1: (pl.ds(0, edge), pl.ds(edge + inner, edge)),
    }
    cur_copies = []
    for turn in range(groups):
        seen = (groups - turn) % groups
        for shift in (1, -1, 0):
            if (shift, turn) == (0, 0):
                continue
            source, target = parts[shift]
            copy = pltpu.make_async_remote_copy(
                src_ref=cur_ref.at[source],
                dst_ref=table.at[seen, target],
                send_sem=cur_send.at[shift + 1, turn],
                recv_sem=cur_recv.at[shift + 1, seen],
                device_id=device(shift, turn),
                device_id_type=pl.DeviceIdType.MESH,
            )
            copy.start()
            cur_copies.append(copy)
    table[0, pl.ds(edge, inner), :] = cur_ref[...]

    row = iota((boxes * rows_box, inner), 0)
    column = iota((boxes * rows_box, inner), 1)
    wanted = ((row >> 3) << 1) + (row & 7)
    spread[...] = dot(one_hot((column == wanted) & ((row & 7) < 2)), cur_ref[...])

    def coarse_step(step, carry):
        for i in range(4):
            box = step * 4 + i
            at = pl.ds(pl.multiple_of(box * rows_box, rows_box), rows_box)
            coarse_sum[at, :] = dot_t(
                spread[at, :].astype(half), rad[box].reshape(2 * lane, lane)
            )
        return carry

    for q in range(rad_chunks):
        rad_copies[q].wait()
        lax.fori_loop(q * rad_step // 4, (q + 1) * rad_step // 4, coarse_step, 0)
    coarse = (coarse_sum[:, :lane] + turned(coarse_sum[:, lane:])).astype(half)

    count = span * 2 * cap
    per = 2 * cap
    row = iota((count, peers), 0)
    target = lax.rem(place + row // per - reach + peers, peers)
    listed = dot(one_hot(iota((count, peers), 1) == target), list_ref[...].astype(full).astype(half))
    row = iota((count, cap), 0)
    listed = jnp.sum(
        jnp.where(iota((count, cap), 1) == row % cap, listed, 0.0), axis=1, keepdims=True
    )
    row = iota((count, 1), 0)
    listed = listed.astype(jnp.int32) * rows_box + (row % per) // cap
    chosen = dot(one_hot(iota((count, boxes * rows_box), 1) == listed), coarse)
    outgoing[...] = chosen.astype(half).reshape(outgoing.shape)
    pat_copies = []
    for shift, turn in others:
        seen = (groups - turn) % groups
        copy = pltpu.make_async_remote_copy(
            src_ref=outgoing.at[shift + reach],
            dst_ref=arrived.at[seen, reach - shift],
            send_sem=pat_send.at[turn, shift + reach],
            recv_sem=pat_recv.at[seen, reach - shift],
            device_id=device(shift, turn),
            device_id_type=pl.DeviceIdType.MESH,
        )
        copy.start()
        pat_copies.append(copy)
    arrived[0, reach] = outgoing[reach]

    slots[...] = jnp.full(slots.shape, -1, jnp.int32)
    kinds[...] = jnp.full(kinds.shape, -1, jnp.int32)
    own_rows = pl.ds(pl.multiple_of(first, 8), mine)
    slots[:, :entries] = slot_ref[own_rows, :] - (place - reach) * cap
    kinds[:, :entries] = kind_ref[own_rows, :]
    live, kind_rows = counts.shape[1], counts.shape[2]

    def count_step(step, carry):
        for i in range(2):
            box = step * 2 + i
            slot_row = slots[pl.ds(box, 1), :]
            kind_row = kinds[pl.ds(box, 1), :]
            wide = slots.shape[1]
            by_slot = one_hot(iota((live, wide), 0) == slot_row)
            by_kind = one_hot(iota((kind_rows, wide), 0) == kind_row)
            counts[box] = dot_t(by_slot, by_kind).astype(half)
        return carry

    lax.fori_loop(0, mine // 2, count_step, 0)

    for copy in cur_copies:
        copy.wait()
    row = iota((mine * rows_box, mine), 0)
    moves = dot(
        one_hot(iota((mine * rows_box, mine), 1) == (row >> 3)),
        off_ref[own_rows, :].astype(full).astype(half),
    ).astype(jnp.int32)
    row = iota((mine * rows_box, 1), 0)
    turn, part = (row & 7) >> 1, row & 1
    flat = table[...].reshape(groups * table_rows, lane)
    near_count = moves.shape[1]
    for n in range(near_count):
        position = first + (row >> 3) + moves[:, n : n + 1]
        whole = place * boxes + position
        valid = (whole >= 0) & (whole < peers * boxes) & (turn < groups)
        index = jnp.where(valid, turn * table_rows + (position + rim) * 2 + part, -1)
        picked = one_hot(iota((mine * rows_box, groups * table_rows), 1) == index)
        src[:, n * lane : (n + 1) * lane] = dot(picked, flat)

    def near_step_of(box, carry):
        at = pl.ds(pl.multiple_of(box * rows_box, rows_box), rows_box)
        block = jnp.concatenate(
            [near[box, n].reshape(2 * lane, lane) for n in range(near_count)], axis=1
        )
        near_sum[at, :] = dot_t(src[at, :].astype(half), block)
        return carry

    for q in range(near_chunks):
        near_copies[q].wait()
        lax.fori_loop(q * near_step, (q + 1) * near_step, near_step_of, 0, unroll=2)

    for copy in pat_copies:
        copy.wait()
    for turn in range(groups):
        for part in range(2):
            got = arrived[turn, :, part].reshape(live, lane)
            pats[turn, part] = dot_t(got, interp_ref[...]).astype(half).astype(full)

    trans_copy.wait()
    for j in range(blocks):
        lanes = slice(j * lane, (j + 1) * lane)

        def translate(step, carry):
            start = step * batch
            mixed = dot(
                counts[pl.ds(start, batch)].reshape(batch * live, kind_rows), trans[j]
            ).reshape(batch, live, 2 * lane)
            for i in range(batch):
                real, imag = mixed[i, :, :lane], mixed[i, :, lane:]
                sums = []
                for turn in range(groups):
                    pat_real, pat_imag = pats[turn, 0, :, lanes], pats[turn, 1, :, lanes]
                    sums.append(
                        jnp.sum(real * pat_real - imag * pat_imag, axis=0, keepdims=True)
                    )
                    sums.append(
                        jnp.sum(real * pat_imag + imag * pat_real, axis=0, keepdims=True)
                    )
                if len(sums) < rows_box:
                    sums.append(jnp.zeros((rows_box - len(sums), lane), full))
                at = pl.ds(pl.multiple_of((start + i) * rows_box, rows_box), rows_box)
                inc[at, lanes] = jnp.concatenate(sums, axis=0)
            return carry

        lax.fori_loop(0, mine // batch, translate, 0)

    back[...] = dot(inc[...].astype(half), interp_ref[...])

    def far_step(step, carry):
        for i in range(4):
            box = step * 4 + i
            at = pl.ds(pl.multiple_of(box * rows_box, rows_box), rows_box)
            block = jnp.concatenate([rad[first + box, 0], rad[first + box, 1]], axis=1)
            far_sum[at, :] = dot(back[at, :].astype(half), block)
        return carry

    lax.fori_loop(0, mine // 4, far_step, 0)
    total = (
        near_sum[:, :lane]
        + far_sum[:, :lane]
        + turned(near_sum[:, lane:] - far_sum[:, lane:])
    ).astype(half)
    row = iota((2 * mine, mine * rows_box), 0)
    column = iota((2 * mine, mine * rows_box), 1)
    for turn in range(groups):
        picked = one_hot(column == (row >> 1) * rows_box + 2 * turn + (row & 1))
        stage[turn] = dot(picked, total).astype(half)
    res_copies = []
    for turn in range(1, groups):
        copy = pltpu.make_async_remote_copy(
            src_ref=stage.at[turn],
            dst_ref=result.at[group],
            send_sem=res_send.at[turn],
            recv_sem=res_recv.at[groups - turn],
            device_id=device(0, turn),
            device_id_type=pl.DeviceIdType.MESH,
        )
        copy.start()
        res_copies.append(copy)
    result[group] = stage[0]
    for copy in res_copies:
        copy.wait()
    out_ref[...] = result[...].reshape(out_ref.shape)


def on_device(
    currents, near_blocks, near_off, radiation, interp, translators, send_list, inter_slot, trans_id
):
    groups, peers = lax.axis_size("groups"), lax.axis_size("box")
    boxes, size = currents.shape[0], currents.shape[2]
    mine = boxes // groups
    samples, cap = interp.shape[0], send_list.shape[2]
    blocks = samples // lane
    kind_count = translators.shape[0]
    kind_rows = -(-kind_count // lane) * lane
    wide = -(-inter_slot.shape[1] // lane) * lane
    live = span * cap
    near_count = near_off.shape[1]
    tiles = jnp.transpose(
        translators.astype(half).reshape(kind_count, 2, blocks, lane), (2, 0, 1, 3)
    ).reshape(blocks, kind_count, 2 * lane)
    tiles = jnp.pad(tiles, ((0, 0), (0, kind_rows - kind_count), (0, 0)))
    near_chunks, rad_chunks = 4, 4
    inside = pl.BlockSpec(memory_space=pltpu.VMEM)
    outside = pl.BlockSpec(memory_space=pl.ANY)
    out = pl.pallas_call(
        functools.partial(kernel, groups, peers, near_chunks, rad_chunks, 4),
        out_shape=jax.ShapeDtypeStruct((2 * boxes, size), half),
        in_specs=[inside, outside, inside, outside, inside, outside, inside, inside, inside],
        out_specs=inside,
        scratch_shapes=[
            pltpu.VMEM((mine,) + near_blocks.shape[1:], half),
            pltpu.VMEM(radiation.shape, half),
            pltpu.VMEM(tiles.shape, half),
            pltpu.VMEM((groups, 4 * boxes, size), half),
            pltpu.VMEM((mine * rows_box, near_count * size), full),
            pltpu.VMEM((mine * rows_box, 2 * size), full),
            pltpu.VMEM((mine * rows_box, 2 * size), full),
            pltpu.VMEM((boxes * rows_box, size), full),
            pltpu.VMEM((boxes * rows_box, 2 * size), full),
            pltpu.VMEM((span, 2, cap, lane), half),
            pltpu.VMEM((groups, span, 2, cap, lane), half),
            pltpu.VMEM((mine, live, kind_rows), half),
            pltpu.VMEM((groups, 2, live, samples), full),
            pltpu.VMEM((mine, wide), jnp.int32),
            pltpu.VMEM((mine, wide), jnp.int32),
            pltpu.VMEM((mine * rows_box, samples), full),
            pltpu.VMEM((mine * rows_box, lane), full),
            pltpu.VMEM((groups, 2 * mine, size), half),
            pltpu.VMEM((groups, 2 * mine, size), half),
            pltpu.SemaphoreType.DMA((near_chunks,)),
            pltpu.SemaphoreType.DMA((rad_chunks,)),
            pltpu.SemaphoreType.DMA,
            pltpu.SemaphoreType.DMA((3, groups)),
            pltpu.SemaphoreType.DMA((3, groups)),
            pltpu.SemaphoreType.DMA((groups, span)),
            pltpu.SemaphoreType.DMA((groups, span)),
            pltpu.SemaphoreType.DMA((groups,)),
            pltpu.SemaphoreType.DMA((groups,)),
        ],
        compiler_params=pltpu.CompilerParams(
            collective_id=0, has_side_effects=True, vmem_limit_bytes=50 * 2**20
        ),
    )(
        currents.reshape(2 * boxes, size), near_blocks, near_off, radiation, interp, tiles,
        send_list.reshape(send_list.shape[1:]), inter_slot, trans_id,
    )
    return out.reshape(currents.shape)


def solution(mesh):
    return jax.shard_map(
        on_device,
        mesh=mesh,
        in_specs=(
            P(("groups", "box"), None, None),
            P("box", None, None, None, None),
            P("box", None),
            P("box", None, None, None),
            P(),
            P(),
            P("box", None, None),
            P("box", None),
            P("box", None),
        ),
        out_specs=P(("groups", "box"), None, None),
        check_vma=False,
    )
```

time: 440 us -> 38.1 us (0.09)
  other arithmetic: 212 us -> 1.75 us
  local copies, waits for them, and re-layouts: 164 us -> 1.51 us
  starting transfers between devices: 36.3 us -> 0 us
  Pallas kernels: 0 us -> 34.6 us
  matrix products: 14.7 us -> 0 us
  waiting for transfers between devices: 8.16 us -> 0 us
    gather x17 -> x0, local copies, waits for them, and re-layouts: 158 us -> none  [the longest x7 78.1 us: translate(): shifts = translators[kinds]]
    reduce_sum x7 -> x0, other arithmetic: 156 us -> none  [translate(): jnp.sum(shifts[:, :, 0] * pats[:, :, 0] - shifts[:, :, 1] * pats[:, :, 1]...]
    convert_element_type x9 -> x0, other arithmetic: 51.1 us -> none  [the longest x7 51 us: translate(): pats = received[slots].astype(jnp.float32)]
    ppermute x14 -> x0, starting transfers between devices: 36.3 us -> none  [the longest x12 32 us: shifted(): lax.ppermute(value, axis, [(source, source + steps) for source in range(l...]
    pallas_call x0 -> x1, Pallas kernels: none -> 34.6 us  [on_device(): pl.pallas_call(functools.partial(kernel, groups, peers, near_chunks, rad_...]
    dot_general x5 -> x0, matrix products: 14.7 us -> none  [the longest x1 8.08 us: on_device(): jnp.einsum('bncij,bnej->bcei', near_blocks, sources, preferred_element_ty...]
    ppermute x14 -> x0, waiting for transfers between devices: 8.16 us -> none  [the longest x12 7.64 us: shifted(): lax.ppermute(value, axis, [(source, source + steps) for source in range(l...]
  transfers between devices with their start and end apart: 14 -> 0, of which waited for: 2 -> 0; matrix products, arithmetic and copies ran while one was open for 4% -> 0% of each run, Pallas kernels for 0% -> 0%
where the time goes in v1:
time: 38.1 us; the launch traced here: 38 us
  Pallas kernels  34.6 us (91%)
  other arithmetic  1.75 us (5%)
  local copies, waits for them, and re-layouts  1.51 us (4%)
    pallas_call x1, Pallas kernels, on_device(): pl.pallas_call(functools.partial(kernel, groups, peers, near_chunks, rad_...  34.6 us
    transpose x1, other arithmetic, on_device(): jnp.transpose(translators.astype(half).reshape(kind_count, 2, blocks, lan...  1.75 us
    unnamed x14, local copies, waits for them, and re-layouts  1.04 us

profile of v1, /device:TPU:0, one launch (start us, length us, event | category | flops | bytes accessed | tf_op | source)
XLA Modules:
  0.0 38.0 jit_solution(192511565907259896)
XLA Ops:
  0.0 1.8 %bitcast_bitcast_fusion = bf16[4,316,2,128]{3,2,1,0:T(2,128)(2,1)S(1)} fusion(f32[316,2,512]{2,1,0:T(2,128)} %param.14), kind=kLoop, calls=%fused_computation | loop fusion | flops 323584 | bytes 1941504 | tf_op jit(solution)/shard_map/transpose | solution.py:307
  1.8 0.0 copy-start.5
  1.8 0.0 copy-start
  1.8 0.0 copy-start.1
  1.8 0.0 copy-start.2
  1.8 0.0 copy-start.3
  1.8 0.0 copy-start.4
  1.8 0.4 %reshape.17 = bf16[4,316,256]{2,1,0:T(8,128)(2,1)S(1)} reshape(bf16[4,316,2,128]{3,2,1,0:T(2,128)(2,1)S(1)} %bitcast_bitcast_fusion) | data formatting | bytes 1294336 | tf_op jit(solution)/shard_map/reshape | solution.py:309
  2.2 0.1 pad.4.trans_hbm
  2.3 0.1 copy-done.5
  2.4 0.1 copy.13.off_ref
  2.5 0.1 copy-done
  2.7 0.0 copy-done.1
  2.7 0.0 copy-done.2
  2.7 0.0 copy-done.3
  2.7 0.0 copy-done.4
  2.7 34.6 %shard_map.91 = bf16[128,128]{1,0:T(8,128)(2,1)S(1)} custom-call(bf16[128,128]{1,0:T(8,128)(2,1)S(1)} %bitcast.11, bf16[64,4,2,128,128]{4,3,2,1,0:T(8,128)(2,1)} %near_hbm.1, s32[64,4]{1,0:T(8,128)S(1)} %copy.13.off_ref, bf16[64,2,128,128]{3,2,1,0:T(8,128)(2,1)} %rad_hbm.1, bf16[512,128]{1,0:T(8,128)(2,1)S(1)} %copy-done, ...), custom_call_target="tpu_custom_call" | custom-call | tf_op jit(solution)/shard_map/pallas_call | solution.py:314
  37.3 0.6 %copy.17 = bf16[64,2,128]{2,1,0:T(2,128)(2,1)} copy(bf16[64,2,128]{2,1,0:T(2,128)(2,1)S(1)} %bitcast.10) | data formatting | bytes 65536
Async XLA Ops:
  1.8 0.7 %copy-start.5 = (s32[64,4]{0,1:T(4,128)S(1)}, s32[64,4]{0,1:T(4,128)}, u32[]{:S(2)}) copy-start(s32[64,4]{0,1:T(4,128)} %param.11) | copy-start | bytes 3076
  1.8 0.9 %copy-start = (bf16[512,128]{1,0:T(8,128)(2,1)S(1)}, bf16[512,128]{1,0:T(8,128)(2,1)}, u32[]{:S(2)}) copy-start(bf16[512,128]{1,0:T(8,128)(2,1)} %interp_ref.1) | copy-start | bytes 393220
  1.8 0.9 %copy-start.1 = (s32[64,189]{1,0:T(8,128)S(1)}, s32[64,189]{1,0:T(8,128)}, u32[]{:S(2)}) copy-start(s32[64,189]{1,0:T(8,128)} %slot_ref.1) | copy-start | bytes 145156
  1.8 0.9 %copy-start.2 = (s32[64,189]{1,0:T(8,128)S(1)}, s32[64,189]{1,0:T(8,128)}, u32[]{:S(2)}) copy-start(s32[64,189]{1,0:T(8,128)} %kind_ref.1) | copy-start | bytes 145156
  1.8 0.9 %copy-start.3 = (bf16[64,2,128]{2,1,0:T(2,128)(2,1)S(1)}, bf16[64,2,128]{2,1,0:T(2,128)(2,1)}, u32[]{:S(2)}) copy-start(bf16[64,2,128]{2,1,0:T(2,128)(2,1)} %param.9) | copy-start | bytes 98308
  1.8 0.9 %copy-start.4 = (s32[1,16,16]{2,1,0:T(8,128)S(1)}, s32[1,16,16]{2,1,0:T(8,128)}, u32[]{:S(2)}) copy-start(s32[1,16,16]{2,1,0:T(8,128)} %param.15) | copy-start | bytes 3076

commit v2 on v1

--- a/solution.py
+++ b/solution.py
@@ -40,8 +40,8 @@
     groups, peers, near_chunks, rad_chunks, batch,
     cur_ref, near_hbm, off_ref, rad_hbm, interp_ref, trans_hbm, list_ref, slot_ref, kind_ref,
     out_ref,
-    near, rad, trans, table, src, near_sum, far_sum, spread, coarse_sum, outgoing, arrived,
-    counts, pats, slots, kinds, inc, back, stage, result,
+    near, rad, raw, trans, table, src, near_sum, far_sum, spread, coarse_sum, outgoing, arrived,
+    counts, marks, mixed_even, mixed_odd, pats, slots, kinds, inc, back, stage, result,
     near_sem, rad_sem, trans_sem, cur_send, cur_recv, pat_send, pat_recv, res_send, res_recv,
 ):
     group, place = lax.axis_index("groups"), lax.axis_index("box")
@@ -87,9 +87,34 @@
         )
         for q in range(near_chunks)
     ]
-    trans_copy = pltpu.make_async_copy(trans_hbm, trans, trans_sem)
+    trans_copy = pltpu.make_async_copy(trans_hbm, raw, trans_sem)
     for copy in rad_copies + [trans_copy] + near_copies:
         copy.start()
+
+    live, kind_rows = counts.shape[1], counts.shape[2]
+    wide = slots.shape[1]
+    marks[...] = (iota(marks.shape, 0) - lane).astype(full).astype(half)
+    slots[...] = jnp.full(slots.shape, -1.0 - lane, full)
+    kinds[...] = jnp.full(kinds.shape, -1.0 - lane, full)
+    own_rows = pl.ds(pl.multiple_of(first, 8), mine)
+    slots[:, :entries] = (slot_ref[own_rows, :] - (place - reach) * cap - lane).astype(full)
+    kinds[:, :entries] = (kind_ref[own_rows, :] - lane).astype(full)
+    one, none = jnp.ones((), half), jnp.zeros((), half)
+
+    def matches(numbers, box, rows):
+        line = jnp.broadcast_to(numbers[pl.ds(box, 1), :], (16, wide)).astype(half)
+        line = jnp.broadcast_to(line[None], (rows // 16, 16, wide)).reshape(rows, wide)
+        return jnp.where(marks[:rows, :] == line, one, none)
+
+    def count_step(step, carry):
+        for i in range(4):
+            box = step * 4 + i
+            counts[box] = dot_t(
+                matches(slots, box, live), matches(kinds, box, kind_rows)
+            ).astype(half)
+        return carry
+
+    lax.fori_loop(0, mine // 4, count_step, 0)
 
     pl.semaphore_wait(barrier, len(others))
 
@@ -166,32 +191,12 @@
         pat_copies.append(copy)
     arrived[0, reach] = outgoing[reach]
 
-    slots[...] = jnp.full(slots.shape, -1, jnp.int32)
-    kinds[...] = jnp.full(kinds.shape, -1, jnp.int32)
-    own_rows = pl.ds(pl.multiple_of(first, 8), mine)
-    slots[:, :entries] = slot_ref[own_rows, :] - (place - reach) * cap
-    kinds[:, :entries] = kind_ref[own_rows, :]
-    live, kind_rows = counts.shape[1], counts.shape[2]
-
-    def count_step(step, carry):
-        for i in range(2):
-            box = step * 2 + i
-            slot_row = slots[pl.ds(box, 1), :]
-            kind_row = kinds[pl.ds(box, 1), :]
-            wide = slots.shape[1]
-            by_slot = one_hot(iota((live, wide), 0) == slot_row)
-            by_kind = one_hot(iota((kind_rows, wide), 0) == kind_row)
-            counts[box] = dot_t(by_slot, by_kind).astype(half)
-        return carry
-
-    lax.fori_loop(0, mine // 2, count_step, 0)
-
     for copy in cur_copies:
         copy.wait()
-    row = iota((mine * rows_box, mine), 0)
-    moves = dot(
-        one_hot(iota((mine * rows_box, mine), 1) == (row >> 3)),
-        off_ref[own_rows, :].astype(full).astype(half),
+    row = iota((mine * rows_box, boxes), 0)
+    moves = dot_t(
+        one_hot(iota((mine * rows_box, boxes), 1) == first + (row >> 3)),
+        off_ref[...].astype(full).astype(half),
     ).astype(jnp.int32)
     row = iota((mine * rows_box, 1), 0)
     turn, part = (row & 7) >> 1, row & 1
@@ -215,44 +220,68 @@
 
     for q in range(near_chunks):
         near_copies[q].wait()
-        lax.fori_loop(q * near_step, (q + 1) * near_step, near_step_of, 0, unroll=2)
+        lax.fori_loop(q * near_step, (q + 1) * near_step, near_step_of, 0, unroll=4)
+
+    trans_copy.wait()
+    kind_count = raw.shape[0] // (2 * blocks)
+    whole_rows = -(-kind_count // 16) * 16
+    for j in range(blocks):
+        for part in range(2):
+            piece = raw[pl.ds(j * 2 + part, kind_count, stride=2 * blocks), :]
+            if whole_rows > kind_count:
+                piece = jnp.concatenate(
+                    [piece, jnp.zeros((whole_rows - kind_count, lane), full)], axis=0
+                )
+            trans[j, :whole_rows, part * lane : (part + 1) * lane] = piece.astype(half)
+        if kind_rows > whole_rows:
+            trans[j, whole_rows:, :] = jnp.zeros((kind_rows - whole_rows, 2 * lane), half)
 
     for copy in pat_copies:
         copy.wait()
     for turn in range(groups):
         for part in range(2):
             got = arrived[turn, :, part].reshape(live, lane)
-            pats[turn, part] = dot_t(got, interp_ref[...]).astype(half).astype(full)
-
-    trans_copy.wait()
-    for j in range(blocks):
-        lanes = slice(j * lane, (j + 1) * lane)
-
-        def translate(step, carry):
-            start = step * batch
-            mixed = dot(
-                counts[pl.ds(start, batch)].reshape(batch * live, kind_rows), trans[j]
-            ).reshape(batch, live, 2 * lane)
-            for i in range(batch):
-                real, imag = mixed[i, :, :lane], mixed[i, :, lane:]
-                sums = []
-                for turn in range(groups):
-                    pat_real, pat_imag = pats[turn, 0, :, lanes], pats[turn, 1, :, lanes]
-                    sums.append(
-                        jnp.sum(real * pat_real - imag * pat_imag, axis=0, keepdims=True)
-                    )
-                    sums.append(
-                        jnp.sum(real * pat_imag + imag * pat_real, axis=0, keepdims=True)
-                    )
-                if len(sums) < rows_box:
-                    sums.append(jnp.zeros((rows_box - len(sums), lane), full))
-                at = pl.ds(pl.multiple_of((start + i) * rows_box, rows_box), rows_box)
-                inc[at, lanes] = jnp.concatenate(sums, axis=0)
-            return carry
-
-        lax.fori_loop(0, mine // batch, translate, 0)
-
-    back[...] = dot(inc[...].astype(half), interp_ref[...])
+            pattern = dot_t(got, interp_ref[...]).astype(half).astype(full)
+            for j in range(blocks):
+                pats[j, turn, part] = pattern[:, j * lane : (j + 1) * lane]
+
+    chunks = mine // batch
+    steps = blocks * chunks
+
+    def mix(step, into):
+        j, chunk = step // chunks, lax.rem(step, chunks)
+        into[...] = dot(
+            counts[pl.ds(chunk * batch, batch)].reshape(batch * live, kind_rows), trans[j]
+        )
+
+    def translate(step, mixed):
+        j, chunk = step // chunks, lax.rem(step, chunks)
+        for i in range(batch):
+            rows = slice(i * live, (i + 1) * live)
+            real, imag = mixed[rows, :lane], mixed[rows, lane:]
+            sums = []
+            for turn in range(groups):
+                pat_real, pat_imag = pats[j, turn, 0], pats[j, turn, 1]
+                sums.append(jnp.sum(real * pat_real - imag * pat_imag, axis=0, keepdims=True))
+                sums.append(jnp.sum(real * pat_imag + imag * pat_real, axis=0, keepdims=True))
+            if len(sums) < rows_box:
+                sums.append(jnp.zeros((rows_box - len(sums), lane), full))
+            at = pl.ds(pl.multiple_of((chunk * batch + i) * rows_box, rows_box), rows_box)
+            inc[j, at, :] = jnp.concatenate(sums, axis=0)
+
+    def pair(step, carry):
+        mix(2 * step + 1, mixed_odd)
+        translate(2 * step, mixed_even)
+        mix(jnp.minimum(2 * step + 2, steps - 1), mixed_even)
+        translate(2 * step + 1, mixed_odd)
+        return carry
+
+    mix(0, mixed_even)
+    lax.fori_loop(0, steps // 2, pair, 0)
+
+    back[...] = dot(
+        jnp.concatenate([inc[j].astype(half) for j in range(blocks)], axis=1), interp_ref[...]
+    )
 
     def far_step(step, carry):
         for i in range(4):
@@ -305,21 +334,22 @@
     live = span * cap
     near_count = near_off.shape[1]
     tiles = jnp.transpose(
-        translators.astype(half).reshape(kind_count, 2, blocks, lane), (2, 0, 1, 3)
-    ).reshape(blocks, kind_count, 2 * lane)
-    tiles = jnp.pad(tiles, ((0, 0), (0, kind_rows - kind_count), (0, 0)))
+        translators.reshape(kind_count, 2, blocks, lane), (0, 2, 1, 3)
+    ).reshape(kind_count * 2 * blocks, lane)
+    batch = 4
     near_chunks, rad_chunks = 4, 4
     inside = pl.BlockSpec(memory_space=pltpu.VMEM)
     outside = pl.BlockSpec(memory_space=pl.ANY)
     out = pl.pallas_call(
-        functools.partial(kernel, groups, peers, near_chunks, rad_chunks, 4),
+        functools.partial(kernel, groups, peers, near_chunks, rad_chunks, batch),
         out_shape=jax.ShapeDtypeStruct((2 * boxes, size), half),
         in_specs=[inside, outside, inside, outside, inside, outside, inside, inside, inside],
         out_specs=inside,
         scratch_shapes=[
             pltpu.VMEM((mine,) + near_blocks.shape[1:], half),
             pltpu.VMEM(radiation.shape, half),
-            pltpu.VMEM(tiles.shape, half),
+            pltpu.VMEM(tiles.shape, full),
+            pltpu.VMEM((blocks, kind_rows, 2 * lane), half),
             pltpu.VMEM((groups, 4 * boxes, size), half),
             pltpu.VMEM((mine * rows_box, near_count * size), full),
             pltpu.VMEM((mine * rows_box, 2 * size), full),
@@ -329,10 +359,13 @@
             pltpu.VMEM((span, 2, cap, lane), half),
             pltpu.VMEM((groups, span, 2, cap, lane), half),
             pltpu.VMEM((mine, live, kind_rows), half),
-            pltpu.VMEM((groups, 2, live, samples), full),
-            pltpu.VMEM((mine, wide), jnp.int32),
-            pltpu.VMEM((mine, wide), jnp.int32),
-            pltpu.VMEM((mine * rows_box, samples), full),
+            pltpu.VMEM((kind_rows, wide), half),
+            pltpu.VMEM((batch * live, 2 * lane), full),
+            pltpu.VMEM((batch * live, 2 * lane), full),
+            pltpu.VMEM((blocks, groups, 2, live, lane), full),
+            pltpu.VMEM((mine, wide), full),
+            pltpu.VMEM((mine, wide), full),
+            pltpu.VMEM((blocks, mine * rows_box, lane), full),
             pltpu.VMEM((mine * rows_box, lane), full),
             pltpu.VMEM((groups, 2 * mine, size), half),
             pltpu.VMEM((groups, 2 * mine, size), half),
@@ -350,7 +383,7 @@
             collective_id=0, has_side_effects=True, vmem_limit_bytes=50 * 2**20
         ),
     )(
-        currents.reshape(2 * boxes, size), near_blocks, near_off, radiation, interp, tiles,
+        currents.reshape(2 * boxes, size), near_blocks, near_off.T, radiation, interp, tiles,
         send_list.reshape(send_list.shape[1:]), inter_slot, trans_id,
     )
     return out.reshape(currents.shape)

time: 38.1 us -> 36.1 us (0.948)
  Pallas kernels: 34.6 us -> 29.1 us
  local copies, waits for them, and re-layouts: 1.51 us -> 6.64 us
  other arithmetic: 1.75 us -> 0 us
    unnamed x14 -> x15, local copies, waits for them, and re-layouts: 1.04 us -> 6.64 us
    pallas_call x1, Pallas kernels: 34.6 us -> 29.1 us  [on_device(): pl.pallas_call(functools.partial(kernel, groups, peers, near_chunks, rad_...]
    transpose x1 -> x0, other arithmetic: 1.75 us -> none  [on_device(): jnp.transpose(translators.astype(half).reshape(kind_count, 2, blocks, lan...]
    reshape x1 -> x0, local copies, waits for them, and re-layouts: 0.41 us -> none  [on_device(): tiles = jnp.transpose(translators.astype(half).reshape(kind_count, 2, blo...]
where the time goes in v2:
time: 36.1 us; the launch traced here: 35.7 us
  Pallas kernels  29.1 us (81%)
  local copies, waits for them, and re-layouts  6.64 us (18%)
    pallas_call x1, Pallas kernels, on_device(): pl.pallas_call(functools.partial(kernel, groups, peers, near_chunks, rad_...  29.1 us
    unnamed x15, local copies, waits for them, and re-layouts  6.64 us

profile of v2, /device:TPU:0, one launch (start us, length us, event | category | flops | bytes accessed | tf_op | source)
XLA Modules:
  0.0 35.7 jit_solution(12981698609508243102)
XLA Ops:
  0.0 0.0 copy-start
  0.0 1.3 %copy-done = f32[316,2,512]{2,1,0:T(2,128)S(1)} copy-done((f32[316,2,512]{2,1,0:T(2,128)S(1)}, f32[316,2,512]{2,1,0:T(2,128)}, u32[]{:S(2)}) %copy-start) | copy-done | bytes 1294360
  1.3 0.0 copy-start.1
  1.3 0.9 %copy-done.1 = bf16[512,128]{1,0:T(8,128)(2,1)S(1)} copy-done((bf16[512,128]{1,0:T(8,128)(2,1)S(1)}, bf16[512,128]{1,0:T(8,128)(2,1)}, u32[]{:S(2)}) %copy-start.1) | copy-done | bytes 131096
  2.2 0.0 copy-start.2
  2.2 0.8 %copy-done.2 = s32[64,189]{1,0:T(8,128)S(1)} copy-done((s32[64,189]{1,0:T(8,128)S(1)}, s32[64,189]{1,0:T(8,128)}, u32[]{:S(2)}) %copy-start.2) | copy-done | bytes 48408
  3.1 0.0 copy-start.3
  3.1 0.8 %copy-done.3 = s32[64,189]{1,0:T(8,128)S(1)} copy-done((s32[64,189]{1,0:T(8,128)S(1)}, s32[64,189]{1,0:T(8,128)}, u32[]{:S(2)}) %copy-start.3) | copy-done | bytes 48408
  3.9 0.0 copy-start.4
  3.9 0.8 %copy-done.4 = bf16[64,2,128]{2,1,0:T(2,128)(2,1)S(1)} copy-done((bf16[64,2,128]{2,1,0:T(2,128)(2,1)S(1)}, bf16[64,2,128]{2,1,0:T(2,128)(2,1)}, u32[]{:S(2)}) %copy-start.4) | copy-done | bytes 32792
  4.7 0.0 copy-start.5
  4.7 0.7 %copy-done.5 = s32[1,16,16]{2,1,0:T(8,128)S(1)} copy-done((s32[1,16,16]{2,1,0:T(8,128)S(1)}, s32[1,16,16]{2,1,0:T(8,128)}, u32[]{:S(2)}) %copy-start.5) | copy-done | bytes 1048
  5.4 0.0 copy-start.6
  5.4 0.7 %copy-done.6 = s32[64,4]{0,1:T(4,128)S(1)} copy-done((s32[64,4]{0,1:T(4,128)S(1)}, s32[64,4]{0,1:T(4,128)}, u32[]{:S(2)}) %copy-start.6) | copy-done | bytes 1048
  6.0 29.1 %shard_map.91 = bf16[128,128]{1,0:T(8,128)(2,1)S(1)} custom-call(bf16[128,128]{1,0:T(8,128)(2,1)S(1)} %bitcast.11, bf16[64,4,2,128,128]{4,3,2,1,0:T(8,128)(2,1)} %near_hbm.1, s32[4,64]{1,0:T(4,128)S(1)} %bitcast.13, bf16[64,2,128,128]{3,2,1,0:T(8,128)(2,1)} %rad_hbm.1, bf16[512,128]{1,0:T(8,128)(2,1)S(1)} %copy-done.1, f32[2528,128]{1,0:T(8,128)S(1)} %bitcast.9, ...), custom_call_target="tpu_custom_call" | custom-call | tf_op jit(solution)/shard_map/pallas_call | solution.py:343
  35.1 0.6 %copy.12 = bf16[64,2,128]{2,1,0:T(2,128)(2,1)} copy(bf16[64,2,128]{2,1,0:T(2,128)(2,1)S(1)} %bitcast.10) | data formatting | bytes 65536
Async XLA Ops:
  0.0 1.3 %copy-start = (f32[316,2,512]{2,1,0:T(2,128)S(1)}, f32[316,2,512]{2,1,0:T(2,128)}, u32[]{:S(2)}) copy-start(f32[316,2,512]{2,1,0:T(2,128)} %param.14) | copy-start | bytes 3883012
  1.3 0.9 %copy-start.1 = (bf16[512,128]{1,0:T(8,128)(2,1)S(1)}, bf16[512,128]{1,0:T(8,128)(2,1)}, u32[]{:S(2)}) copy-start(bf16[512,128]{1,0:T(8,128)(2,1)} %interp_ref.1) | copy-start | bytes 393220
  2.2 0.8 %copy-start.2 = (s32[64,189]{1,0:T(8,128)S(1)}, s32[64,189]{1,0:T(8,128)}, u32[]{:S(2)}) copy-start(s32[64,189]{1,0:T(8,128)} %slot_ref.1) | copy-start | bytes 145156
  3.1 0.8 %copy-start.3 = (s32[64,189]{1,0:T(8,128)S(1)}, s32[64,189]{1,0:T(8,128)}, u32[]{:S(2)}) copy-start(s32[64,189]{1,0:T(8,128)} %kind_ref.1) | copy-start | bytes 145156
  3.9 0.8 %copy-start.4 = (bf16[64,2,128]{2,1,0:T(2,128)(2,1)S(1)}, bf16[64,2,128]{2,1,0:T(2,128)(2,1)}, u32[]{:S(2)}) copy-start(bf16[64,2,128]{2,1,0:T(2,128)(2,1)} %param.9) | copy-start | bytes 98308
  4.7 0.7 %copy-start.5 = (s32[1,16,16]{2,1,0:T(8,128)S(1)}, s32[1,16,16]{2,1,0:T(8,128)}, u32[]{:S(2)}) copy-start(s32[1,16,16]{2,1,0:T(8,128)} %param.15) | copy-start | bytes 3076
  5.4 0.7 %copy-start.6 = (s32[64,4]{0,1:T(4,128)S(1)}, s32[64,4]{0,1:T(4,128)}, u32[]{:S(2)}) copy-start(s32[64,4]{0,1:T(4,128)} %param.11) | copy-start | bytes 3076

commit v3 on v2

--- a/solution.py
+++ b/solution.py
@@ -38,11 +38,12 @@
 
 def kernel(
     groups, peers, near_chunks, rad_chunks, batch,
-    cur_ref, near_hbm, off_ref, rad_hbm, interp_ref, trans_hbm, list_ref, slot_ref, kind_ref,
+    cur_hbm, near_hbm, off_hbm, rad_hbm, interp_hbm, trans_hbm, list_hbm, slot_hbm, kind_hbm,
     out_ref,
+    slot_ref, kind_ref, cur_ref, list_ref, off_ref, interp_ref,
     near, rad, raw, trans, table, src, near_sum, far_sum, spread, coarse_sum, outgoing, arrived,
     counts, marks, mixed_even, mixed_odd, pats, slots, kinds, inc, back, stage, result,
-    near_sem, rad_sem, trans_sem, cur_send, cur_recv, pat_send, pat_recv, res_send, res_recv,
+    small_sem, near_sem, rad_sem, trans_sem, cur_send, cur_recv, pat_send, pat_recv, res_send, res_recv,
 ):
     group, place = lax.axis_index("groups"), lax.axis_index("box")
     boxes = rad.shape[0]
@@ -70,6 +71,13 @@
             barrier, inc=1, device_id=device(shift, turn), device_id_type=pl.DeviceIdType.MESH
         )
 
+    small_copies = [
+        pltpu.make_async_copy(source, target, small_sem.at[i])
+        for i, (source, target) in enumerate([
+            (slot_hbm, slot_ref), (kind_hbm, kind_ref), (cur_hbm, cur_ref),
+            (list_hbm, list_ref), (off_hbm, off_ref), (interp_hbm, interp_ref),
+        ])
+    ]
     rad_step, near_step = boxes // rad_chunks, mine // near_chunks
     rad_copies = [
         pltpu.make_async_copy(
@@ -88,7 +96,7 @@
         for q in range(near_chunks)
     ]
     trans_copy = pltpu.make_async_copy(trans_hbm, raw, trans_sem)
-    for copy in rad_copies + [trans_copy] + near_copies:
+    for copy in small_copies + rad_copies + [trans_copy] + near_copies:
         copy.start()
 
     live, kind_rows = counts.shape[1], counts.shape[2]
@@ -97,6 +105,8 @@
     slots[...] = jnp.full(slots.shape, -1.0 - lane, full)
     kinds[...] = jnp.full(kinds.shape, -1.0 - lane, full)
     own_rows = pl.ds(pl.multiple_of(first, 8), mine)
+    small_copies[0].wait()
+    small_copies[1].wait()
     slots[:, :entries] = (slot_ref[own_rows, :] - (place - reach) * cap - lane).astype(full)
     kinds[:, :entries] = (kind_ref[own_rows, :] - lane).astype(full)
     one, none = jnp.ones((), half), jnp.zeros((), half)
@@ -116,6 +126,8 @@
 
     lax.fori_loop(0, mine // 4, count_step, 0)
 
+    for copy in small_copies[2:]:
+        copy.wait()
     pl.semaphore_wait(barrier, len(others))
 
     inner = 2 * boxes
@@ -336,16 +348,22 @@
     tiles = jnp.transpose(
         translators.reshape(kind_count, 2, blocks, lane), (0, 2, 1, 3)
     ).reshape(kind_count * 2 * blocks, lane)
-    batch = 4
+    batch = 8
     near_chunks, rad_chunks = 4, 4
     inside = pl.BlockSpec(memory_space=pltpu.VMEM)
-    outside = pl.BlockSpec(memory_space=pl.ANY)
+    outside = pl.BlockSpec(memory_space=pltpu.HBM)
     out = pl.pallas_call(
         functools.partial(kernel, groups, peers, near_chunks, rad_chunks, batch),
         out_shape=jax.ShapeDtypeStruct((2 * boxes, size), half),
-        in_specs=[inside, outside, inside, outside, inside, outside, inside, inside, inside],
+        in_specs=[outside] * 9,
         out_specs=inside,
         scratch_shapes=[
+            pltpu.VMEM(inter_slot.shape, jnp.int32),
+            pltpu.VMEM(trans_id.shape, jnp.int32),
+            pltpu.VMEM((2 * boxes, size), half),
+            pltpu.VMEM(send_list.shape[1:], jnp.int32),
+            pltpu.VMEM((near_count, boxes), jnp.int32),
+            pltpu.VMEM(interp.shape, half),
             pltpu.VMEM((mine,) + near_blocks.shape[1:], half),
             pltpu.VMEM(radiation.shape, half),
             pltpu.VMEM(tiles.shape, full),
@@ -369,6 +387,7 @@
             pltpu.VMEM((mine * rows_box, lane), full),
             pltpu.VMEM((groups, 2 * mine, size), half),
             pltpu.VMEM((groups, 2 * mine, size), half),
+            pltpu.SemaphoreType.DMA((6,)),
             pltpu.SemaphoreType.DMA((near_chunks,)),
             pltpu.SemaphoreType.DMA((rad_chunks,)),
             pltpu.SemaphoreType.DMA,
@@ -380,7 +399,7 @@
             pltpu.SemaphoreType.DMA((groups,)),
         ],
         compiler_params=pltpu.CompilerParams(
-            collective_id=0, has_side_effects=True, vmem_limit_bytes=50 * 2**20
+            collective_id=0, has_side_effects=True, vmem_limit_bytes=60 * 2**20
         ),
     )(
         currents.reshape(2 * boxes, size), near_blocks, near_off.T, radiation, interp, tiles,

time: 36.1 us -> 30.9 us (0.86)
  local copies, waits for them, and re-layouts: 6.64 us -> 1.4 us
    unnamed x15 -> x1, local copies, waits for them, and re-layouts: 6.64 us -> 1.4 us
where the time goes in v3:
time: 30.9 us; the launch traced here: 30.7 us
  Pallas kernels  29.3 us (95%)
  local copies, waits for them, and re-layouts  1.4 us (5%)
    pallas_call x1, Pallas kernels, on_device(): pl.pallas_call(functools.partial(kernel, groups, peers, near_chunks, rad_...  29.3 us
    unnamed x1, local copies, waits for them, and re-layouts  1.4 us

profile of v3, /device:TPU:0, one launch (start us, length us, event | category | flops | bytes accessed | tf_op | source)
XLA Modules:
  0.0 30.7 jit_solution(4535360889451317904)
XLA Ops:
  0.0 29.3 %shard_map.91 = bf16[128,128]{1,0:T(8,128)(2,1)} custom-call(bf16[128,128]{1,0:T(8,128)(2,1)} %bitcast.11, bf16[64,4,2,128,128]{4,3,2,1,0:T(8,128)(2,1)} %near_hbm.1, s32[4,64]{1,0:T(4,128)} %bitcast.13, bf16[64,2,128,128]{3,2,1,0:T(8,128)(2,1)} %rad_hbm.1, bf16[512,128]{1,0:T(8,128)(2,1)} %interp_hbm.1, f32[2528,128]{1,0:T(8,128)} %bitcast.9, ...), custom_call_target="tpu_custom_call" | custom-call | tf_op jit(solution)/shard_map/pallas_call | solution.py:355
  29.3 1.4 %copy.12 = bf16[64,2,128]{2,1,0:T(2,128)(2,1)} copy(bf16[64,2,128]{2,1,0:T(2,128)(2,1)} %bitcast.10) | data formatting | bytes 65536

commit v4 on v3

--- a/solution.py
+++ b/solution.py
@@ -117,14 +117,14 @@
         return jnp.where(marks[:rows, :] == line, one, none)
 
     def count_step(step, carry):
-        for i in range(4):
-            box = step * 4 + i
+        for i in range(8):
+            box = step * 8 + i
             counts[box] = dot_t(
                 matches(slots, box, live), matches(kinds, box, kind_rows)
             ).astype(half)
         return carry
 
-    lax.fori_loop(0, mine // 4, count_step, 0)
+    lax.fori_loop(0, mine // 8, count_step, 0)
 
     for copy in small_copies[2:]:
         copy.wait()
@@ -162,8 +162,8 @@
     spread[...] = dot(one_hot((column == wanted) & ((row & 7) < 2)), cur_ref[...])
 
     def coarse_step(step, carry):
-        for i in range(4):
-            box = step * 4 + i
+        for i in range(8):
+            box = step * 8 + i
             at = pl.ds(pl.multiple_of(box * rows_box, rows_box), rows_box)
             coarse_sum[at, :] = dot_t(
                 spread[at, :].astype(half), rad[box].reshape(2 * lane, lane)
@@ -172,7 +172,7 @@
 
     for q in range(rad_chunks):
         rad_copies[q].wait()
-        lax.fori_loop(q * rad_step // 4, (q + 1) * rad_step // 4, coarse_step, 0)
+        lax.fori_loop(q * rad_step // 8, (q + 1) * rad_step // 8, coarse_step, 0)
     coarse = (coarse_sum[:, :lane] + turned(coarse_sum[:, lane:])).astype(half)
 
     count = span * 2 * cap
@@ -232,7 +232,7 @@
 
     for q in range(near_chunks):
         near_copies[q].wait()
-        lax.fori_loop(q * near_step, (q + 1) * near_step, near_step_of, 0, unroll=4)
+        lax.fori_loop(q * near_step, (q + 1) * near_step, near_step_of, 0, unroll=min(8, near_step))
 
     trans_copy.wait()
     kind_count = raw.shape[0] // (2 * blocks)
@@ -296,14 +296,14 @@
     )
 
     def far_step(step, carry):
-        for i in range(4):
-            box = step * 4 + i
+        for i in range(8):
+            box = step * 8 + i
             at = pl.ds(pl.multiple_of(box * rows_box, rows_box), rows_box)
             block = jnp.concatenate([rad[first + box, 0], rad[first + box, 1]], axis=1)
             far_sum[at, :] = dot(back[at, :].astype(half), block)
         return carry
 
-    lax.fori_loop(0, mine // 4, far_step, 0)
+    lax.fori_loop(0, mine // 8, far_step, 0)
     total = (
         near_sum[:, :lane]
         + far_sum[:, :lane]

time: 30.9 us -> 29.5 us (0.955)
  Pallas kernels: 29.3 us -> 28 us
    pallas_call x1, Pallas kernels: 29.3 us -> 28 us  [on_device(): pl.pallas_call(functools.partial(kernel, groups, peers, near_chunks, rad_...]
where the time goes in v4:
time: 29.5 us; the launch traced here: 29.4 us
  Pallas kernels  28 us (95%)
  local copies, waits for them, and re-layouts  1.4 us (5%)
    pallas_call x1, Pallas kernels, on_device(): pl.pallas_call(functools.partial(kernel, groups, peers, near_chunks, rad_...  28 us
    unnamed x1, local copies, waits for them, and re-layouts  1.4 us

profile of v4, /device:TPU:0, one launch (start us, length us, event | category | flops | bytes accessed | tf_op | source)
XLA Modules:
  0.0 29.4 jit_solution(10454206700018048636)
XLA Ops:
  0.0 28.0 %shard_map.91 = bf16[128,128]{1,0:T(8,128)(2,1)} custom-call(bf16[128,128]{1,0:T(8,128)(2,1)} %bitcast.11, bf16[64,4,2,128,128]{4,3,2,1,0:T(8,128)(2,1)} %near_hbm.1, s32[4,64]{1,0:T(4,128)} %bitcast.13, bf16[64,2,128,128]{3,2,1,0:T(8,128)(2,1)} %rad_hbm.1, bf16[512,128]{1,0:T(8,128)(2,1)} %interp_hbm.1, f32[2528,128]{1,0:T(8,128)} %bitcast.9, ...), custom_call_target="tpu_custom_call" | custom-call | tf_op jit(solution)/shard_map/pallas_call | solution.py:355
  28.0 1.4 %copy.12 = bf16[64,2,128]{2,1,0:T(2,128)(2,1)} copy(bf16[64,2,128]{2,1,0:T(2,128)(2,1)} %bitcast.10) | data formatting | bytes 65536
